TPU v7x, 32 devices: a whole 2x2x4 slice. The times are simulated.
32 devices in a mesh: groups: 2 (over y), ctx: 4 (over z), head: 2 (over x), sub: 2 (over core).
Axes of the slice: x: 2, y: 2, z: 4, core: 2. Of those that a mesh axis runs over, the one named last changes fastest.
Arguments:
- inputs: bfloat16 [4096, 2048], P(('groups', 'ctx')), parts along dimension 0, may hold values from -1.5 to 1.5
- w_in: bfloat16 [2048, 4096], P(None, 'head'), may hold values from -0.125 to 0.125
- b_in: bfloat16 [4096, 128], P(('groups', 'ctx'), 'sub'), parts along dimension 0, may hold values from -6 to 6
- c_in: bfloat16 [4096, 128], P(('groups', 'ctx'), 'sub'), parts along dimension 0, may hold values from -6 to 6
- log_decay: float32 [64, 4096], P('head', ('groups', 'ctx')), parts along dimension 1, as said below
- level_weight: float32 [3, 64, 4096], P(None, 'head', ('groups', 'ctx')), parts along dimension 2, may hold values from 0.2 to 1
- out_grad: bfloat16 [4096, 4096], P(('groups', 'ctx'), 'head'), parts along dimension 0, may hold values from -0.03125 to 0.03125
Outputs:
- grad_inputs: bfloat16 [4096, 2048], P(('groups', 'ctx'), ('head', 'sub')), parts along dimension 0
- grad_b: bfloat16 [4096, 128], P(('groups', 'ctx', 'head'), 'sub'), parts along dimension 0
- grad_c: bfloat16 [4096, 128], P(('groups', 'ctx', 'head'), 'sub'), parts along dimension 0
There are 2 independent parts, one for each index of `groups`. A program takes and returns all parts, laid end to end along the dimension named above; an argument that names none is the same for every part. Nothing has to cross between parts.
Inputs may be any that keep to these rules, and one draw needn't show every extreme that they name: `log_decay`: each entry is negative.
All inputs are finite; a program needn't handle non-finite values.
Results may differ from a plain program's by a relative error of at most 0.015.
Values may be sent and summed in bfloat16 or wider, within the bound.
A program may use at most 128 MiB of HBM per device.

v0:
```python
import jax
import jax.numpy as jnp
from jax import lax
from jax.sharding import PartitionSpec as P

highest = lax.Precision.HIGHEST


def passed_along(x, axis, by):
    count = lax.axis_size(axis)
    pairs = [(i, i + by) for i in range(count) if 0 <= i + by < count]
    return lax.ppermute(x, axis, pairs)


def shortened(x):

    def short(part):
        return part.astype(jnp.bfloat16) if part.dtype == jnp.float32 else part

    return jax.tree.map(short, x)


def shards(inputs, w_in, b_in, c_in, log_decay, level_weight, out_grad):
    tok_rows = inputs.shape[0]
    head_group = log_decay.shape[0]
    inner_width = w_in.shape[1]
    head_width = inner_width // head_group
    state_part = b_in.shape[1]
    level_count = lax.axis_size("ctx").bit_length() - 1
    projected = jnp.dot(inputs, w_in, preferred_element_type=jnp.float32).astype(jnp.bfloat16)
    proj_heads = projected.reshape(tok_rows, head_group, head_width)
    grad_heads = out_grad.reshape(tok_rows, head_group, head_width)
    proj_f32 = proj_heads.astype(jnp.float32)
    grad_f32 = grad_heads.astype(jnp.float32)
    b_f32 = b_in.astype(jnp.float32)
    c_f32 = c_in.astype(jnp.float32)
    cumulative = jnp.cumsum(log_decay, axis=1)
    block_total = cumulative[:, -1]
    end_weight = jnp.exp(block_total[:, None] - cumulative)
    end_state = jnp.einsum("hu,un,uhp->hnp", end_weight, b_f32, proj_f32, precision=highest)
    flat_size = state_part * head_width
    arrived_list, gap_list, window_list = ([], [], [])
    gap_log = jnp.zeros_like(block_total)
    window_state = end_state
    window_log = block_total
    for level_idx in range(level_count):
        arrived_flat, arrived_log = (
            passed_along(
                window_state.reshape(head_group, flat_size).astype(jnp.bfloat16),
                "ctx",
                2**level_idx,
            ).astype(jnp.float32),
            passed_along(window_log.astype(jnp.bfloat16), "ctx", 2**level_idx).astype(
                window_log.dtype
            ),
        )
        arrived = arrived_flat.reshape(head_group, state_part, head_width)
        arrived_list.append(arrived)
        gap_list.append(gap_log)
        window_list.append(window_log)
        window_state = window_state + jnp.exp(window_log)[:, None, None] * arrived
        window_log = window_log + arrived_log
        gap_log = gap_log + arrived_log
    inter_c = jnp.zeros((tok_rows, state_part), jnp.float32)
    arrived_grads = []
    for level_idx in range(level_count):
        level_coef = level_weight[level_idx + 1] * jnp.exp(
            cumulative + gap_list[level_idx][:, None]
        )
        arrived_grads.append(
            jnp.einsum("ht,tn,thp->hnp", level_coef, c_f32, grad_f32, precision=highest)
        )
        inter_c = inter_c + jnp.einsum(
            "ht,hnp,thp->tn", level_coef, arrived_list[level_idx], grad_f32, precision=highest
        )
    state_grad = jnp.zeros_like(end_state)
    for level_idx in reversed(range(level_count)):
        returned = (
            arrived_grads[level_idx] + jnp.exp(window_list[level_idx])[:, None, None] * state_grad
        )
        came_back = passed_along(
            shortened(returned.reshape(head_group, flat_size)), "ctx", -(2**level_idx)
        )
        state_grad = state_grad + came_back.reshape(head_group, state_part, head_width)
    positions = jnp.arange(tok_rows)
    causal = positions[:, None] >= positions[None, :]
    log_gap = cumulative[:, :, None] - cumulative[:, None, :]
    mask_decay = jnp.where(causal, jnp.exp(jnp.where(causal, log_gap, 0.0)), 0.0)
    scores = jnp.dot(c_in, b_in.T, preferred_element_type=jnp.float32)
    pair_dots = jnp.einsum(
        "thp,uhp->htu", grad_heads, proj_heads, preferred_element_type=jnp.float32
    )
    lam_local = level_weight[0]
    z_total = jnp.sum(mask_decay * lam_local[:, :, None] * pair_dots, axis=0)
    z_round = z_total.astype(jnp.bfloat16)
    local_weight = (mask_decay * scores[None] * lam_local[:, :, None]).astype(jnp.bfloat16)
    grad_x = jnp.einsum(
        "htu,thp->uhp", local_weight, grad_heads, preferred_element_type=jnp.float32
    )
    grad_x = grad_x + jnp.einsum("hu,hnp,un->uhp", end_weight, state_grad, b_f32, precision=highest)
    grad_b = lax.dot_general(
        z_round, c_in, (((0,), (0,)), ((), ())), preferred_element_type=jnp.float32
    )
    grad_b = grad_b + jnp.einsum(
        "hu,hnp,uhp->un", end_weight, state_grad, proj_f32, precision=highest
    )
    grad_c = jnp.dot(z_round, b_in, preferred_element_type=jnp.float32) + inter_c
    summed_b, summed_c = (
        lax.psum_scatter(
            grad_b.astype(jnp.bfloat16), "head", scatter_dimension=0, tiled=True
        ).astype(jnp.float32),
        lax.psum_scatter(
            grad_c.astype(jnp.bfloat16), "head", scatter_dimension=0, tiled=True
        ).astype(jnp.float32),
    )
    grad_flat = grad_x.reshape(tok_rows, inner_width)
    model_width = w_in.shape[0]
    head_share = model_width // lax.axis_size("head")
    out_cols = head_share // lax.axis_size("sub")
    grad_full = lax.psum(grad_flat.astype(jnp.bfloat16), "sub")
    reduced = lax.psum_scatter(
        lax.dot_general(
            w_in, grad_full, (((1,), (1,)), ((), ())), preferred_element_type=jnp.float32
        ).astype(jnp.bfloat16),
        "head",
        scatter_dimension=0,
        tiled=True,
    ).astype(jnp.float32)
    own_cols = lax.dynamic_slice_in_dim(reduced, lax.axis_index("sub") * out_cols, out_cols, 0)
    grad_inputs = own_cols.T.astype(jnp.bfloat16)
    return (grad_inputs, summed_b.astype(jnp.bfloat16), summed_c.astype(jnp.bfloat16))


def solution(mesh):
    in_specs = (
        P(("groups", "ctx"), None),
        P(None, "head"),
        P(("groups", "ctx"), "sub"),
        P(("groups", "ctx"), "sub"),
        P("head", ("groups", "ctx")),
        P(None, "head", ("groups", "ctx")),
        P(("groups", "ctx"), "head"),
    )
    out_specs = (
        P(("groups", "ctx"), ("head", "sub")),
        P(("groups", "ctx", "head"), "sub"),
        P(("groups", "ctx", "head"), "sub"),
    )
    return jax.shard_map(shards, mesh=mesh, in_specs=in_specs, out_specs=out_specs, check_vma=False)
```

profile of v0, /device:TPU:0, one launch (start us, length us, event | category | flops | bytes accessed | tf_op | source)
XLA Modules:
  0.0 200.5 jit_solution(8179085309552300429)
XLA Ops:
  9.9 4.9 %collective-permute-start = (bf16[32]{0:T(256)(128)(2,1)S(1)}, bf16[32]{0:T(256)(128)(2,1)S(1)}, u32[]{:S(2)}, u32[]{:S(2)}) collective-permute-start(bf16[32]{0:T(256)(128)(2,1)S(1)} %convert_element_type.92), channel_id=1, source_target_pairs={{0,4},{4,8},{8,12},{1,5},{5,9},{9,13},{2,6},{6,10},{10,14},{3,7},{... | collective-permute-start | bytes 200 | tf_op jit(solution)/shard_map/ppermute | solution.py:12
  14.8 3.9 %copy.30 = bf16[512,2048]{0,1:T(8,128)(2,1)} copy(bf16[512,2048]{1,0:T(8,128)(2,1)} %param.13) | data formatting | bytes 4194304 | tf_op args[6]
  18.8 9.1 %convolution_convert_fusion = bf16[512,2048]{1,0:T(8,128)(2,1)} fusion(bf16[512,2048]{1,0:T(8,128)(2,1)S(1)} %copy-done, bf16[2048,2048]{1,0:T(8,128)(2,1)} %param.8), kind=kOutput, calls=%fused_computation.26 | convolution fusion | flops 4296015872 | bytes 12582912 | tf_op jit(solution)/shard_map/dot_general | solution.py:30
  27.9 4.0 %copy.33 = bf16[512,2048]{0,1:T(8,128)(2,1)} copy(bf16[512,2048]{1,0:T(8,128)(2,1)} %convolution_convert_fusion) | data formatting | bytes 4194304 | tf_op jit(solution)/shard_map/convert_element_type | solution.py:30
  33.3 3.7 %add_convert_fusion.3 = bf16[32,64,64]{2,1,0:T(8,128)(2,1)S(1)} fusion(f32[32]{0:T(128)S(1)} %get-tuple-element.9, bf16[512,32,64]{0,2,1:T(8,128)(2,1)} %bitcast.102, f32[512,64]{0,1:T(8,128)S(1)} %convert.14, f32[512,32]{0,1:T(8,128)S(1)} %get-tuple-element.4), kind=kOutput, calls=%fused_computation.51 | convolution fusion | flops 806617088 | bytes 2556032 | tf_op jit(solution)/shard_map/ht,tn,thp->hnp/dot_general | solution.py:71
  37.5 1.3 collective-permute-start.1
  38.8 4.7 %fusion.59 = (bf16[32,64,64]{2,1,0:T(8,128)(2,1)S(1)}, f32[32,64,64]{2,1,0:T(8,128)}) fusion(bf16[512,32,64]{0,2,1:T(8,128)(2,1)} %bitcast.99, f32[512,64]{0,1:T(8,128)S(1)} %convert.13, f32[512,32]{0,1:T(8,128)S(1)} %get-tuple-element.5), kind=kOutput, calls=%fused_computation.74 | convolution fusion | flops 806486016 | bytes 3080192 | tf_op jit(solution)/shard_map/hu,un,uhp->hnp/dot_general | solution.py:40
  44.6 4.2 %collective-permute-start.3 = (bf16[32,4096]{1,0:T(8,128)(2,1)}, bf16[32,4096]{1,0:T(8,128)(2,1)}, u32[]{:S(2)}, u32[]{:S(2)}) collective-permute-start(bf16[32,4096]{1,0:T(8,128)(2,1)} %convert_element_type.114), channel_id=1, source_target_pairs={{0,4},{4,8},{8,12},{1,5},{5,9},{9,13},{2,6},{6,10},{10,14},{3,7},{... | collective-permute-start | bytes 786440 | tf_op jit(solution)/shard_map/ppermute | solution.py:12
  49.6 1.4 fusion.60
  51.0 2.8 %collective-permute-done.1 = bf16[32,4096]{1,0:T(8,128)(2,1)} collective-permute-done((bf16[32,4096]{1,0:T(8,128)(2,1)S(1)}, bf16[32,4096]{1,0:T(8,128)(2,1)}, u32[]{:S(2)}, u32[]{:S(2)}) %collective-permute-start.1) | collective-permute-done | bytes 262176 | tf_op jit(solution)/shard_map/ppermute | solution.py:12
  53.8 1.4 reshape.87
  55.1 2.3 %reshape.84 = bf16[32,64,64]{2,1,0:T(8,128)(2,1)} reshape(bf16[32,4096]{1,0:T(8,128)(2,1)} %collective-permute-done.3) | data formatting | bytes 524288 | tf_op jit(solution)/shard_map/reshape | solution.py:57
  57.4 5.0 %add_convert_fusion.1 = (bf16[32,64,64]{2,1,0:T(8,128)(2,1)}, bf16[32,64,64]{2,1,0:T(8,128)(2,1)}) fusion(f32[32,64,64]{2,1,0:T(8,128)} %get-tuple-element.11, bf16[32,64,64]{2,1,0:T(8,128)(2,1)} %reshape.84, f32[32]{0:T(128)S(1)} %get-tuple-element.8, f32[32,64,64]{2,1,0:T(8,128)S(1)} %reshape.87, bf16[512,32,64]{0,2,1:T(8,128)(2,1)} %bitcast.103, ...), kind=kOutput, calls=%fused_computation.48 | convolution fusion | flops 807272448 | bytes 4128896 | tf_op jit(solution)/shard_map/ht,tn,thp->hnp/dot_general | solution.py:71
  62.4 2.2 %convert_element_type.99 = bf16[32,4096]{1,0:T(8,128)(2,1)} reshape(bf16[32,64,64]{2,1,0:T(8,128)(2,1)} %get-tuple-element.7) | data formatting | bytes 524288 | tf_op jit(solution)/shard_map/convert_element_type | solution.py:18
  65.9 13.5 %fusion.1 = f32[32,512,64]{1,2,0:T(8,128)} fusion(bf16[512,32,64]{0,2,1:T(8,128)(2,1)} %bitcast.104, f32[32,512]{1,0:T(8,128)} %slice_bitcast_fusion, f32[512,512]{0,1:T(8,128)} %fusion.60, f32[32,512]{1,0:T(8,128)} %copy-done.5, pred[512,512]{0,1:T(8,128)(4,1)} %iota_compare_fusion), kind=kOutput, calls=%fused_computation.4 | convolution fusion | flops 1124073472 | bytes 7733248 | tf_op jit(solution)/shard_map/htu,thp->uhp/dot_general | solution.py:97
  79.4 2.4 %reshape.88 = f32[32,64,64]{2,1,0:T(8,128)} reshape(bf16[32,4096]{1,0:T(8,128)(2,1)} %collective-permute-done.2) | data formatting | bytes 786432 | tf_op jit(solution)/shard_map/convert_element_type | solution.py:84
  81.8 7.4 %add_convert_fusion = bf16[32,512,64]{1,2,0:T(8,128)(2,1)} fusion(f32[32,512,64]{1,2,0:T(8,128)} %fusion.1, f32[512,64]{0,1:T(8,128)S(1)} %convert.13, f32[512,32]{0,1:T(8,128)S(1)} %get-tuple-element.5, f32[32,64,64]{2,1,0:T(8,128)S(1)} %reshape.87, f32[32,64,64]{2,1,0:T(8,128)} %reshape.88), kind=kOutput, calls=%fused_computation.23 | convolution fusion | flops 808583168 | bytes 7536640 | tf_op jit(solution)/shard_map/hu,hnp,un->uhp/dot_general | solution.py:100
  89.5 24.9 %all-reduce.2.cloned.1.call-done = bf16[512,2048]{0,1:T(8,128)(2,1)} async-done(((bf16[512,2048]{0,1:T(8,128)(2,1)}), bf16[512,2048]{0,1:T(8,128)(2,1)}) %all-reduce.2.cloned.1.call-update) | async-done | bytes 2097168 | tf_op jit(solution)/shard_map/psum | solution.py:120
  114.3 9.9 %fusion.20 = bf16[2048,512]{0,1:T(8,128)(2,1)} fusion(bf16[512,2048]{0,1:T(8,128)(2,1)} %all-reduce.2.cloned.1.call-done, bf16[2048,2048]{1,0:T(8,128)(2,1)} %param.8), kind=kOutput, calls=%fused_computation.28 | convolution fusion | flops 4296015872 | bytes 12582912 | tf_op jit(solution)/shard_map/dot_general | solution.py:122
  124.3 16.1 %fusion = bf16[512,512]{0,1:T(8,128)(2,1)} fusion(f32[32,512]{1,0:T(8,128)S(1)} %copy-done.7, f32[32,512]{1,0:T(8,128)S(1)} %copy-done.6, pred[512,512]{0,1:T(8,128)(4,1)} %iota_compare_fusion, bf16[512,32,64]{0,2,1:T(8,128)(2,1)} %bitcast.100, bf16[512,32,64]{0,2,1:T(8,128)(2,1)} %bitcast.105), kind=kOutput, calls=%fused_computation.1 | convolution fusion | flops 1123811328 | bytes 5111808 | tf_op jit(solution)/shard_map/thp,uhp->htu/dot_general | solution.py:90
  140.5 2.2 %convert_element_type.116 = bf16[32,4096]{1,0:T(8,128)(2,1)} reshape(bf16[32,64,64]{2,1,0:T(8,128)(2,1)} %get-tuple-element.6) | data formatting | bytes 524288 | tf_op jit(solution)/shard_map/convert_element_type | solution.py:49
  142.7 5.3 %collective-permute-start.4 = (bf16[32,4096]{1,0:T(8,128)(2,1)}, bf16[32,4096]{1,0:T(8,128)(2,1)}, u32[]{:S(2)}, u32[]{:S(2)}) collective-permute-start(bf16[32,4096]{1,0:T(8,128)(2,1)} %convert_element_type.116), channel_id=1, source_target_pairs={{0,8},{4,12},{1,9},{5,13},{2,10},{6,14},{3,11},{7,15},{16,24},{20,... | collective-permute-start | bytes 786440 | tf_op jit(solution)/shard_map/ppermute | solution.py:12
  147.9 1.9 fusion.61
  149.8 1.3 fusion.62
  151.2 2.4 %collective-permute-done.4 = bf16[32,4096]{1,0:T(8,128)(2,1)} collective-permute-done((bf16[32,4096]{1,0:T(8,128)(2,1)}, bf16[32,4096]{1,0:T(8,128)(2,1)}, u32[]{:S(2)}, u32[]{:S(2)}) %collective-permute-start.4) | collective-permute-done | bytes 262176 | tf_op jit(solution)/shard_map/ppermute | solution.py:12
  153.6 2.3 %reshape.86 = bf16[32,64,64]{2,1,0:T(8,128)(2,1)} reshape(bf16[32,4096]{1,0:T(8,128)(2,1)} %collective-permute-done.4) | data formatting | bytes 524288 | tf_op jit(solution)/shard_map/reshape | solution.py:57
  155.9 3.7 %fusion.34 = f32[512,64]{0,1:T(8,128)S(1)} fusion(bf16[32,64,64]{2,1,0:T(8,128)(2,1)} %reshape.86, bf16[512,32,64]{0,2,1:T(8,128)(2,1)} %bitcast.106, f32[512,32]{0,1:T(8,128)} %copy-done.8), kind=kOutput, calls=%fused_computation.40 | convolution fusion | flops 807403520 | bytes 2555904 | tf_op jit(solution)/shard_map/ht,hnp,thp->tn/dot_general | solution.py:73
  159.6 4.4 %fusion.47 = bf16[512,64]{0,1:T(8,128)(2,1)} fusion(f32[512,64]{0,1:T(8,128)} %fusion.61, f32[512,64]{0,1:T(8,128)S(1)} %fusion.34, bf16[32,64,64]{2,1,0:T(8,128)(2,1)} %reshape.84, bf16[512,32,64]{0,2,1:T(8,128)(2,1)} %bitcast.107, f32[512,32]{0,1:T(8,128)S(1)} %get-tuple-element.3), kind=kOutput, calls=%fused_computation.47 | convolution fusion | flops 807501824 | bytes 2752512 | tf_op jit(solution)/shard_map/ht,hnp,thp->tn/dot_general | solution.py:73
  164.0 5.6 %fusion.44 = bf16[512,64]{0,1:T(8,128)(2,1)} fusion(f32[512,64]{0,1:T(8,128)S(1)} %fusion.62, bf16[512,32,64]{0,2,1:T(8,128)(2,1)} %bitcast.101, f32[512,32]{0,1:T(8,128)S(1)} %get-tuple-element.5, f32[32,64,64]{2,1,0:T(8,128)S(1)} %reshape.87, f32[32,64,64]{2,1,0:T(8,128)} %reshape.88), kind=kOutput, calls=%fused_computation.46 | convolution fusion | flops 807600128 | bytes 3407872 | tf_op jit(solution)/shard_map/hu,hnp,uhp->un/dot_general | solution.py:104
  169.7 1.9 fusion.48
  171.6 9.9 %reduce-scatter.8.cloned.1.call-done = bf16[256,64]{0,1:T(8,128)(2,1)} async-done(((bf16[512,64]{0,1:T(8,128)(2,1)}), bf16[256,64]{0,1:T(8,128)(2,1)}) %reduce-scatter.8.cloned.1.call-update) | async-done | bytes 32784 | tf_op jit(solution)/shard_map/reduce_scatter | solution.py:112
  181.5 12.5 %reduce-scatter.6.cloned.1.call-done = bf16[256,64]{0,1:T(8,128)(2,1)} async-done(((bf16[512,64]{0,1:T(8,128)(2,1)}), bf16[256,64]{0,1:T(8,128)(2,1)}) %reduce-scatter.6.cloned.1.call-update) | async-done | bytes 32784 | tf_op jit(solution)/shard_map/reduce_scatter | solution.py:109
  (48 shorter events, 8.2 us)
Async XLA Ops:
  7.2 11.6 %copy-start = (bf16[512,2048]{1,0:T(8,128)(2,1)S(1)}, bf16[512,2048]{1,0:T(8,128)(2,1)}, u32[]{:S(2)}) copy-start(bf16[512,2048]{1,0:T(8,128)(2,1)} %param.7) | copy-start | bytes 6291460
  7.2 11.6 %copy-start.2 = (bf16[512,64]{0,1:T(8,128)(2,1)S(1)}, bf16[512,64]{0,1:T(8,128)(2,1)}, u32[]{:S(2)}) copy-start(bf16[512,64]{0,1:T(8,128)(2,1)} %param.10) | copy-start | bytes 196612
  7.2 107.2 %all-reduce.2.cloned.1.call-start = ((), (), s32[]{:S(2)}) async-start(), calls=%async_computation.3 | async-start | bytes 4194304 | tf_op jit(solution)/shard_map/psum | solution.py:120
  9.7 5.1 %copy-start.5 = (f32[32,512]{1,0:T(8,128)}, f32[32,512]{1,0:T(8,128)S(1)}, u32[]{:S(2)}) copy-start(f32[32,512]{1,0:T(8,128)S(1)} %copy_bitcast_fusion) | copy-start | bytes 196612
  9.9 22.7 %collective-permute-start = (bf16[32]{0:T(256)(128)(2,1)S(1)}, bf16[32]{0:T(256)(128)(2,1)S(1)}, u32[]{:S(2)}, u32[]{:S(2)}) collective-permute-start(bf16[32]{0:T(256)(128)(2,1)S(1)} %convert_element_type.92), channel_id=1, source_target_pairs={{0,4},{4,8},{8,12},{1,5},{5,9},{9,13},{2,6},{6,10},{10,14},{3,7},{... | collective-permute-start | bytes 200 | tf_op jit(solution)/shard_map/ppermute | solution.py:12
  18.8 14.0 %copy-start.3 = (f32[512,64]{0,1:T(8,128)}, f32[512,64]{0,1:T(8,128)S(1)}, u32[]{:S(2)}) copy-start(f32[512,64]{0,1:T(8,128)S(1)} %convert.14) | copy-start | bytes 393220
  27.9 4.0 %copy-start.4 = (f32[3,32,512]{2,1,0:T(8,128)S(1)}, f32[3,32,512]{2,1,0:T(8,128)}, u32[]{:S(2)}) copy-start(f32[3,32,512]{2,1,0:T(8,128)} %param.12) | copy-start | bytes 589828
  27.9 4.6 %copy-start.1 = (bf16[512,64]{0,1:T(8,128)(2,1)S(1)}, bf16[512,64]{0,1:T(8,128)(2,1)}, u32[]{:S(2)}) copy-start(bf16[512,64]{0,1:T(8,128)(2,1)} %param.9) | copy-start | bytes 196612
  32.7 0.6 copy-start.8
  37.5 16.3 %collective-permute-start.1 = (bf16[32,4096]{1,0:T(8,128)(2,1)S(1)}, bf16[32,4096]{1,0:T(8,128)(2,1)}, u32[]{:S(2)}, u32[]{:S(2)}) collective-permute-start(bf16[32,4096]{1,0:T(8,128)(2,1)S(1)} %convert_element_type.95), channel_id=1, source_target_pairs={{8,0},{12,4},{9,1},{13,5},{10,2},{14,6},{11,3},{15,7},{24,16},{28,... | collective-permute-start | bytes 786440 | tf_op jit(solution)/shard_map/ppermute | solution.py:12
  44.6 10.5 %collective-permute-start.3 = (bf16[32,4096]{1,0:T(8,128)(2,1)}, bf16[32,4096]{1,0:T(8,128)(2,1)}, u32[]{:S(2)}, u32[]{:S(2)}) collective-permute-start(bf16[32,4096]{1,0:T(8,128)(2,1)} %convert_element_type.114), channel_id=1, source_target_pairs={{0,4},{4,8},{8,12},{1,5},{5,9},{9,13},{2,6},{6,10},{10,14},{3,7},{... | collective-permute-start | bytes 786440 | tf_op jit(solution)/shard_map/ppermute | solution.py:12
  64.6 14.8 %collective-permute-start.2 = (bf16[32,4096]{1,0:T(8,128)(2,1)}, bf16[32,4096]{1,0:T(8,128)(2,1)}, u32[]{:S(2)}, u32[]{:S(2)}) collective-permute-start(bf16[32,4096]{1,0:T(8,128)(2,1)} %convert_element_type.99), channel_id=1, source_target_pairs={{4,0},{8,4},{12,8},{5,1},{9,5},{13,9},{6,2},{10,6},{14,10},{7,3},{... | collective-permute-start | bytes 786440 | tf_op jit(solution)/shard_map/ppermute | solution.py:12
  89.2 35.2 %copy-start.6 = (f32[32,512]{1,0:T(8,128)S(1)}, f32[32,512]{1,0:T(8,128)}, u32[]{:S(2)}) copy-start(f32[32,512]{1,0:T(8,128)} %copy-done.5) | copy-start | bytes 196612
  89.2 35.2 %copy-start.7 = (f32[32,512]{1,0:T(8,128)S(1)}, f32[32,512]{1,0:T(8,128)}, u32[]{:S(2)}) copy-start(f32[32,512]{1,0:T(8,128)} %slice_bitcast_fusion) | copy-start | bytes 196612
  89.2 80.5 %reduce-scatter.4.cloned.1.call-start = ((), (), s32[]{:S(2)}) async-start(), calls=%async_computation.4 | async-start | bytes 3145728 | tf_op jit(solution)/shard_map/reduce_scatter | solution.py:121
  124.3 57.2 %reduce-scatter.8.cloned.1.call-start = ((), (), s32[]{:S(2)}) async-start(), calls=%async_computation.6 | async-start | bytes 98304 | tf_op jit(solution)/shard_map/reduce_scatter | solution.py:112
  142.7 10.9 %collective-permute-start.4 = (bf16[32,4096]{1,0:T(8,128)(2,1)}, bf16[32,4096]{1,0:T(8,128)(2,1)}, u32[]{:S(2)}, u32[]{:S(2)}) collective-permute-start(bf16[32,4096]{1,0:T(8,128)(2,1)} %convert_element_type.116), channel_id=1, source_target_pairs={{0,8},{4,12},{1,9},{5,13},{2,10},{6,14},{3,11},{7,15},{16,24},{20,... | collective-permute-start | bytes 786440 | tf_op jit(solution)/shard_map/ppermute | solution.py:12
  164.0 30.0 %reduce-scatter.6.cloned.1.call-start = ((), (), s32[]{:S(2)}) async-start(), calls=%async_computation.5 | async-start | bytes 98304 | tf_op jit(solution)/shard_map/reduce_scatter | solution.py:109
Sparse Core Ops, SparseCore 0:
  89.3 25.0 all-reduce.1
  124.4 32.9 reduce-scatter.3
  164.1 17.2 reduce-scatter.7
  184.1 9.8 reduce-scatter.5
where the time goes:
time: 201 us
  matrix products  87.7 us (44%)
  waiting for transfers between devices  52.6 us (26%)
  local copies, waits for them, and re-layouts  24.8 us (12%)
  starting transfers between devices  17.3 us (9%)
  between operations  14 us (7%)
  other arithmetic  4.07 us (2%)
    psum x1, waiting for transfers between devices, shards(): grad_full = lax.psum(grad_flat.astype(jnp.bfloat16), 'sub')  24.9 us
    ppermute x5, starting transfers between devices, passed_along(): return lax.ppermute(x, axis, pairs)  16.9 us
    dot_general x1, matrix products, shards(): jnp.einsum('thp,uhp->htu', grad_heads, proj_heads, preferred_element_type...  16.1 us
    dot_general x1, matrix products, shards(): jnp.einsum('htu,thp->uhp', local_weight, grad_heads, preferred_element_ty...  13.5 us
    reduce_scatter x1, waiting for transfers between devices, shards(): lax.psum_scatter(grad_b.astype(jnp.bfloat16), 'head', scatter_dimension=0...  12.5 us
    dot_general x1, matrix products, shards(): lax.dot_general(w_in, grad_full, (((1,), (1,)), ((), ())), preferred_elem...  9.9 us
    reduce_scatter x1, waiting for transfers between devices, shards(): lax.psum_scatter(grad_c.astype(jnp.bfloat16), 'head', scatter_dimension=0...  9.89 us
    dot_general x1, matrix products, shards(): jnp.dot(inputs, w_in, preferred_element_type=jnp.float32)  9.13 us
  transfers between devices with their start and end apart: 9, of which 5 were waited for; matrix products, arithmetic and copies ran while one was open for 40% of the time, Pallas kernels for 0%

commit v1 on v0

v1 whole, which is shorter than its diff:
```python
import functools
import jax
import jax.numpy as jnp
from jax import lax
from jax.experimental import pallas as pl
from jax.experimental.pallas import tpu as pltpu
from jax.sharding import PartitionSpec as P

F32, BF16 = jnp.float32, jnp.bfloat16
MESH = pl.DeviceIdType.MESH
CHUNK = 256


def mm(a, b):
    return lax.dot_general(a, b, (((1,), (0,)), ((), ())), preferred_element_type=F32)


def mm_nt(a, b):
    return lax.dot_general(a, b, (((1,), (1,)), ((), ())), preferred_element_type=F32)


def remote(src, dst, sems, idx, where):
    return pltpu.make_async_remote_copy(
        src_ref=src, dst_ref=dst, send_sem=sems.at[0, idx], recv_sem=sems.at[1, idx],
        device_id=where, device_id_type=MESH)


def kernel(dims, x_hbm, w_hbm, g_hbm, b_ref, c_ref, dec_ref, lw_ref,
           out_ref, gb_ref, gc_ref,
           x_v, wa_v, wb_v, g_v, b_oth, c_oth, b_v, c_v, bt_v, ct_v,
           coef_v, cumc_v, cumr_v, lam_v, wlog, alog, gap,
           gl_v, p_v, pe_v, a_v, e_v, win_s, arr_v, ret_s, came_v, sg_v,
           sc_v, scb_v, z_v, gxl_v, gx_v, part_s, part_r, own_v, gbc_s, gbc_r,
           ld_sem, bc_sem, log_sem, fwd_sem, bwd_sem, gx_sem, part_sem, gbc_sem):
    T, H, HP, HD, NS, NH, NCTX, LV, OC, RB = dims
    half, quarter = T // 2, T // 4
    hpc = CHUNK // HD
    nchunk = HP // CHUNK
    n_half = b_ref.shape[1]
    N = n_half * NS
    tok_own = T // NH
    blk = T // RB
    sub = lax.axis_index("sub")
    ctx = lax.axis_index("ctx")
    head = lax.axis_index("head")
    other = 1 - sub

    def cols(c):
        return pl.ds(pl.multiple_of(c * CHUNK, CHUNK), CHUNK)

    loads = [
        pltpu.make_async_copy(g_hbm.at[:, pl.ds(pl.multiple_of(sub * HP, 128), HP)], g_v, ld_sem.at[0]),
        pltpu.make_async_copy(x_hbm, x_v, ld_sem.at[1]),
        pltpu.make_async_copy(w_hbm.at[:, pl.ds(pl.multiple_of(sub * HP, 128), HP)], wa_v, ld_sem.at[2]),
    ]
    for k in range(NH):
        loads.append(pltpu.make_async_copy(
            w_hbm.at[pl.ds(pl.multiple_of((k * NS + sub) * OC, 128), OC), :], wb_v.at[k], ld_sem.at[3 + k]))
    for ld in loads:
        ld.start()

    barrier = pltpu.get_barrier_semaphore()
    count = NH * NS - 1
    for dh in range(NH):
        for ds in range(NS):
            if dh or ds:
                pl.semaphore_signal(barrier, inc=1, device_id={
                    "head": lax.rem(head + dh, NH), "sub": lax.rem(sub + ds, NS)}, device_id_type=MESH)
    for l in range(LV):
        hop = 2 ** l
        up, down = ctx + hop < NCTX, ctx - hop >= 0
        count = count + up.astype(jnp.int32) + down.astype(jnp.int32)

        @pl.when(up)
        def _():
            pl.semaphore_signal(barrier, inc=1, device_id={"ctx": ctx + hop}, device_id_type=MESH)

        @pl.when(down)
        def _():
            pl.semaphore_signal(barrier, inc=1, device_id={"ctx": ctx - hop}, device_id_type=MESH)
    pl.semaphore_wait(barrier, count)

    bc_copies = [remote(b_ref, b_oth, bc_sem, 0, {"sub": other}), remote(c_ref, c_oth, bc_sem, 1, {"sub": other})]
    for cp in bc_copies:
        cp.start()

    def own_rows(v):
        r = v[:H]
        for k in range(1, NS):
            r = jnp.where(sub == k, v[k * H:(k + 1) * H], r)
        return r

    rows = [own_rows(dec_ref[...])] + [own_rows(lw_ref[l]) for l in range(LV + 1)]
    used = H * len(rows)
    stacked = jnp.concatenate(rows + [jnp.zeros((128 - used, T), F32)], axis=0)
    turned = jnp.transpose(stacked)
    dec_t = turned[:, :H]
    lam_t = turned[:, H:2 * H]
    r_i = lax.broadcasted_iota(jnp.int32, (T, T), 0)
    c_i = lax.broadcasted_iota(jnp.int32, (T, T), 1)
    tri = jnp.where(r_i >= c_i, 1.0, 0.0).astype(BF16)
    d1 = dec_t.astype(BF16)
    rest = dec_t - d1.astype(F32)
    d2 = rest.astype(BF16)
    d3 = (rest - d2.astype(F32)).astype(BF16)
    cum_t = mm(tri, d1) + (mm(tri, d2) + mm(tri, d3))
    cum_r = jnp.transpose(jnp.concatenate([cum_t, jnp.zeros((T, 128 - H), F32)], axis=1))
    for c in range(nchunk):
        cumr_v[c, :hpc] = cum_r[c * hpc:(c + 1) * hpc]
        lam_v[c, :hpc] = rows[1][c * hpc:(c + 1) * hpc]
        cumc_v[c] = cum_t[:, c * hpc:(c + 1) * hpc]
    tot = cum_t[T - 1:T]
    grow = jnp.exp(cum_t)
    coef_v[0] = jnp.exp(jnp.minimum(tot - cum_t, 0.0))
    for l in range(LV):
        coef_v[1 + l] = turned[:, (l + 2) * H:(l + 3) * H] * grow
    ref_a = cum_t[half - 1:half]
    coef_v[1 + LV] = jnp.concatenate([
        jnp.exp(jnp.minimum(ref_a - cum_t[:half], 0.0)),
        lam_t[half:] * jnp.exp(jnp.minimum(cum_t[half:] - ref_a, 0.0))], axis=0)
    pieces = []
    for base in (0, half):
        mid = base + quarter
        ref_b = cum_t[mid - 1:mid]
        pieces.append(jnp.exp(jnp.minimum(ref_b - cum_t[base:mid], 0.0)))
        pieces.append(lam_t[mid:mid + quarter] * jnp.exp(jnp.minimum(cum_t[mid:mid + quarter] - ref_b, 0.0)))
    coef_v[2 + LV] = jnp.concatenate(pieces, axis=0)

    def selector(c, dtype):
        h_i = lax.broadcasted_iota(jnp.int32, (H, CHUNK), 0)
        l_i = lax.broadcasted_iota(jnp.int32, (H, CHUNK), 1)
        return jnp.where(h_i == c * hpc + lax.div(l_i, HD), 1.0, 0.0).astype(dtype)

    def spread(v, c):
        sel = selector(c, BF16)
        hi = v.astype(BF16)
        lo = (v - hi.astype(F32)).astype(BF16)
        return mm(hi, sel) + mm(lo, sel)

    tot8 = jnp.broadcast_to(tot, (8, H))
    t1 = tot8.astype(BF16)
    rest = tot8 - t1.astype(F32)
    t2 = rest.astype(BF16)
    t3 = (rest - t2.astype(F32)).astype(BF16)
    for c in range(nchunk):
        sel = selector(c, BF16)
        wlog[0, :, c * CHUNK:(c + 1) * CHUNK] = mm(t1, sel) + (mm(t2, sel) + mm(t3, sel))
    gap[0] = jnp.zeros((8, HP), F32)

    def shift(l, sign, src, dst, sems, idx):
        hop = sign * 2 ** l
        sends = (ctx + hop < NCTX) & (ctx + hop >= 0)
        gets = (ctx - hop < NCTX) & (ctx - hop >= 0)
        cp = remote(src, dst, sems, idx, {"ctx": ctx + hop})

        def start():
            pl.when(sends)(cp.start)

        def arrive():
            pl.when(gets)(cp.wait_recv)

            @pl.when(jnp.logical_not(gets))
            def _():
                dst[...] = jnp.zeros(dst.shape, dst.dtype)

        def end():
            pl.when(sends)(cp.wait_send)

        return start, arrive, end

    log_moves = [shift(l, 1, wlog.at[l], alog.at[l], log_sem, l) for l in range(LV - 1)]
    fwd = [shift(l, 1, win_s.at[l], arr_v.at[l], fwd_sem, l) for l in range(LV)]
    bwd = [shift(l, -1, ret_s.at[l], came_v.at[l], bwd_sem, l) for l in range(LV)]

    if LV > 1:
        log_moves[0][0]()

    for cp in bc_copies:
        cp.wait_recv()
    b_v[:, :n_half] = b_ref[...]
    b_v[:, n_half:] = b_oth[...]
    c_v[:, :n_half] = c_ref[...]
    c_v[:, n_half:] = c_oth[...]
    bt_v[...] = jnp.transpose(b_v[...].astype(F32)).astype(BF16)
    ct_v[...] = jnp.transpose(c_v[...].astype(F32)).astype(BF16)
    loads[0].wait()

    def level_grads(l):
        @pl.loop(0, nchunk)
        def _(c):
            gl = (g_v[:, cols(c)].astype(F32) * spread(coef_v[1 + l], c)).astype(BF16)
            gl_v[l, :, cols(c)] = gl
            a_v[l, :, cols(c)] = mm(ct_v[...], gl)

    level_grads(LV - 1)
    for l in range(LV - 1):
        log_moves[l][1]()
        gap[l + 1] = gap[l] + alog[l]
        wlog[l + 1] = wlog[l] + alog[l]
        if l + 1 < LV - 1:
            log_moves[l + 1][0]()
    ret_s[LV - 1] = (a_v[LV - 1] * jnp.exp(gap[LV - 1, 0:1])).astype(BF16)
    bwd[LV - 1][0]()

    loads[1].wait()
    loads[2].wait()

    @pl.loop(0, nchunk)
    def _(c):
        proj = mm(x_v[...], wa_v[:, cols(c)]).astype(BF16)
        p_v[:, cols(c)] = proj
        pe = (proj.astype(F32) * spread(coef_v[0], c)).astype(BF16)
        pe_v[:, cols(c)] = pe
        e = mm(bt_v[...], pe)
        e_v[:, cols(c)] = e
        win_s[0, :, cols(c)] = e.astype(BF16)

    fwd[0][0]()
    for l in range(LV - 1):
        level_grads(l)

    sc_v[...] = mm_nt(b_v[...], c_v[...])
    scb_v[...] = sc_v[...].astype(BF16)
    z_v[...] = jnp.zeros((T, T), F32)

    def off_block(c, coef, u0, t0, size):
        us, ts = slice(u0, u0 + size), slice(t0, t0 + size)
        eb = spread(coef_v[coef, us], c)
        ga = (g_v[ts, cols(c)].astype(F32) * spread(coef_v[coef, ts], c)).astype(BF16)
        pb = (p_v[us, cols(c)].astype(F32) * eb).astype(BF16)
        z_v[us, ts] += mm_nt(pb, ga)
        return eb * mm(scb_v[us, ts], ga)

    @pl.loop(0, nchunk)
    def _(c):
        far = off_block(c, 1 + LV, 0, half, half)
        near_a = off_block(c, 2 + LV, 0, quarter, quarter)
        near_b = off_block(c, 2 + LV, half, half + quarter, quarter)
        gxl_v[:half, cols(c)] = far
        gxl_v[:quarter, cols(c)] += near_a
        gxl_v[half:half + quarter, cols(c)] = near_b
        gxl_v[quarter * 3:, cols(c)] = jnp.zeros((quarter, CHUNK), F32)

    state = [None]

    def ladder(l):
        fwd[l][1]()
        keep = e_v[...] if l == 0 else e_v[...]
        e_v[...] = keep + jnp.exp(wlog[l, 0:1]) * arr_v[l].astype(F32)
        win_s[l + 1] = e_v[...].astype(BF16)
        fwd[l + 1][0]()
        k = LV - 1 - l
        bwd[k][1]()
        if l == 0:
            sg_v[...] = came_v[k].astype(F32)
        else:
            sg_v[...] += came_v[k].astype(F32)
        ret_s[k - 1] = (a_v[k - 1] * jnp.exp(gap[k - 1, 0:1])
                        + jnp.exp(wlog[k - 1, 0:1]) * sg_v[...]).astype(BF16)
        bwd[k - 1][0]()

    for l in range(LV - 1):
        ladder(l)

    q_r = lax.broadcasted_iota(jnp.int32, (quarter, quarter), 0)
    q_c = lax.broadcasted_iota(jnp.int32, (quarter, quarter), 1)

    @pl.loop(0, nchunk)
    def _(c):
        keep = q_c >= q_r
        for i in range(4):
            sl = slice(i * quarter, (i + 1) * quarter)
            p_b, g_b = p_v[sl, cols(c)], g_v[sl, cols(c)]
            zsum = z_v[sl, sl]
            locals_x = []
            for j in range(hpc):
                lanes = slice(j * HD, (j + 1) * HD)
                row = cumr_v[c, j:j + 1, sl]
                lam = lam_v[c, j:j + 1, sl]
                col = cumc_v[c, sl, j:j + 1]
                dec = jnp.where(keep, jnp.exp(jnp.minimum(row - col, 0.0)) * lam, 0.0)
                zsum = zsum + dec * mm_nt(p_b[:, lanes], g_b[:, lanes])
                lwt = (dec * sc_v[sl, sl]).astype(BF16)
                locals_x.append(mm(lwt, g_b[:, lanes]))
            z_v[sl, sl] = zsum
            gxl_v[sl, cols(c)] += jnp.concatenate(locals_x, axis=1)

    bwd[0][1]()
    if LV > 1:
        sg_v[...] += came_v[0].astype(F32)
    else:
        sg_v[...] = came_v[0].astype(F32)
    sgb = sg_v[...].astype(BF16)
    came_v[0] = sgb
    gx_copies = []
    for r in range(RB):
        rs = slice(r * blk, (r + 1) * blk)

        @pl.loop(0, nchunk)
        def _(c):
            ew = spread(coef_v[0, rs], c)
            gx = gxl_v[rs, cols(c)] + ew * mm(b_v[rs], came_v[0, :, cols(c)])
            gx_v[sub, rs, cols(c)] = gx.astype(BF16)

        cp = remote(gx_v.at[sub, pl.ds(r * blk, blk)], gx_v.at[sub, pl.ds(r * blk, blk)], gx_sem, r, {"sub": other})
        cp.start()
        gx_copies.append(cp)

    for k in range(NH):
        loads[3 + k].wait()
    part_copies = []
    for r in range(RB):
        rs = slice(r * blk, (r + 1) * blk)
        gx_copies[r].wait_recv()
        for d in range(1, NH):
            k = lax.rem(head + d, NH)

            part = mm_nt(gx_v[0, rs], wb_v[k, :, :HP]) + mm_nt(gx_v[1, rs], wb_v[k, :, HP:])
            part_s[d - 1, rs] = part.astype(BF16)
            cp = remote(part_s.at[d - 1, pl.ds(r * blk, blk)], part_r.at[d - 1, pl.ds(r * blk, blk)],
                        part_sem, (d - 1) * RB + r, {"head": k})
            cp.start()
            part_copies.append(cp)

    fwd[LV - 1][1]()
    gb_all = mm(z_v[...].astype(BF16), c_v[...]) + mm_nt(pe_v[...], came_v[0])
    gc_all = mm(jnp.transpose(z_v[...]).astype(BF16), b_v[...])
    for l in range(LV):
        gc_all = gc_all + mm_nt(gl_v[l], (arr_v[l].astype(F32) * jnp.exp(gap[l, 0:1])).astype(BF16))
    gbc_copies = []
    gbc_s[0, 0] = gb_all[:, :n_half].astype(BF16)
    gbc_s[0, 1] = gc_all[:, :n_half].astype(BF16)
    gbc_s[1, 0] = gb_all[:, n_half:].astype(BF16)
    gbc_s[1, 1] = gc_all[:, n_half:].astype(BF16)
    for dh in range(NH):
        for ds in range(NS):
            if dh or ds:
                k = lax.rem(head + dh, NH)
                n = dh * NS + ds - 1
                cp = remote(gbc_s.at[ds, :, pl.ds(pl.multiple_of(k * tok_own, 16), tok_own)], gbc_r.at[n],
                            gbc_sem, n, {"head": k, "sub": lax.rem(sub + ds, NS)})
                cp.start()
                gbc_copies.append(cp)
    for r in range(RB):
        rs = slice(r * blk, (r + 1) * blk)
        own_v[rs] = mm_nt(gx_v[0, rs], wb_v[head, :, :HP]) + mm_nt(gx_v[1, rs], wb_v[head, :, HP:])
    own_tok = pl.ds(pl.multiple_of(head * tok_own, 16), tok_own)
    gb = gbc_s[0, 0, own_tok].astype(F32)
    gc = gbc_s[0, 1, own_tok].astype(F32)
    for n, cp in enumerate(gbc_copies):
        cp.wait_recv()
        gb = gb + gbc_r[n, 0].astype(F32)
        gc = gc + gbc_r[n, 1].astype(F32)
    gb_ref[...] = gb.astype(BF16)
    gc_ref[...] = gc.astype(BF16)
    for r in range(RB):
        rs = slice(r * blk, (r + 1) * blk)
        acc = own_v[rs]
        for d in range(1, NH):
            part_copies[r * (NH - 1) + d - 1].wait_recv()
            acc = acc + part_r[d - 1, rs].astype(F32)
        out_ref[rs] = acc.astype(BF16)

    for cp in bc_copies + gx_copies + part_copies + gbc_copies:
        cp.wait_send()
    for mv in log_moves + fwd + bwd:
        mv[2]()


def shards(inputs, w_in, b_in, c_in, log_decay, level_weight, out_grad):
    T, D = inputs.shape
    HG, inner = log_decay.shape[0], w_in.shape[1]
    HD = inner // HG
    NS, NH, NCTX = (lax.axis_size(a) for a in ("sub", "head", "ctx"))
    LV = level_weight.shape[0] - 1
    H = HG // NS
    HP = H * HD
    nh = b_in.shape[1]
    N = nh * NS
    OC = D // NH // NS
    RB = 4
    nchunk = HP // CHUNK
    tok_own = T // NH
    dims = (T, H, HP, HD, NS, NH, NCTX, LV, OC, RB)
    V = pltpu.VMEM
    scratch = [
        V((T, D), BF16), V((D, HP), BF16), V((NH, OC, inner), BF16), V((T, HP), BF16),
        V((T, nh), BF16), V((T, nh), BF16), V((T, N), BF16), V((T, N), BF16), V((N, T), BF16), V((N, T), BF16),
        V((LV + 3, T, H), F32), V((nchunk, T, CHUNK // HD), F32), V((nchunk, 8, T), F32), V((nchunk, 8, T), F32),
        V((LV, 8, HP), F32), V((LV, 8, HP), F32), V((LV, 8, HP), F32),
        V((LV, T, HP), BF16), V((T, HP), BF16), V((T, HP), BF16), V((LV, N, HP), F32), V((N, HP), F32),
        V((LV, N, HP), BF16), V((LV, N, HP), BF16), V((LV, N, HP), BF16), V((LV, N, HP), BF16), V((N, HP), F32),
        V((T, T), F32), V((T, T), BF16), V((T, T), F32), V((T, HP), F32), V((NS, T, HP), BF16),
        V((NH - 1, T, OC), BF16), V((NH - 1, T, OC), BF16), V((T, OC), F32),
        V((NS, 2, T, nh), BF16), V((NH * NS - 1, 2, tok_own, nh), BF16),
    ]
    S = pltpu.SemaphoreType.DMA
    scratch += [S((3 + NH,)), S((2, 2)), S((2, LV)), S((2, LV)), S((2, LV)), S((2, RB)),
                S((2, (NH - 1) * RB)), S((2, NH * NS - 1))]
    vm = pl.BlockSpec(memory_space=pltpu.VMEM)
    hb = pl.BlockSpec(memory_space=pl.ANY)
    return pl.pallas_call(
        functools.partial(kernel, dims),
        out_shape=(jax.ShapeDtypeStruct((T, OC), BF16), jax.ShapeDtypeStruct((tok_own, nh), BF16),
                   jax.ShapeDtypeStruct((tok_own, nh), BF16)),
        in_specs=[hb, hb, hb, vm, vm, vm, vm],
        out_specs=(vm, vm, vm),
        scratch_shapes=scratch,
        compiler_params=pltpu.CompilerParams(
            collective_id=0, has_side_effects=True, vmem_limit_bytes=56 * 2 ** 20),
    )(inputs, w_in, out_grad, b_in, c_in, log_decay, level_weight)


def solution(mesh):
    in_specs = (
        P(("groups", "ctx"), None),
        P(None, "head"),
        P(("groups", "ctx"), "sub"),
        P(("groups", "ctx"), "sub"),
        P("head", ("groups", "ctx")),
        P(None, "head", ("groups", "ctx")),
        P(("groups", "ctx"), "head"),
    )
    out_specs = (
        P(("groups", "ctx"), ("head", "sub")),
        P(("groups", "ctx", "head"), "sub"),
        P(("groups", "ctx", "head"), "sub"),
    )
    return jax.shard_map(shards, mesh=mesh, in_specs=in_specs, out_specs=out_specs, check_vma=False)
```

time: 201 us -> 60.4 us (0.30)
  matrix products: 87.7 us -> 0 us
  waiting for transfers between devices: 52.6 us -> 0 us
  Pallas kernels: 0 us -> 50.5 us
  starting transfers between devices: 17.3 us -> 0 us
  local copies, waits for them, and re-layouts: 24.8 us -> 8.15 us
  between operations: 14 us -> 0.64 us
  other arithmetic: 4.07 us -> 0 us
    dot_general x14 -> x0, matrix products: 87.7 us -> none  [the longest x1 16.1 us: shards(): jnp.einsum('thp,uhp->htu', grad_heads, proj_heads, preferred_element_type...]
    pallas_call x0 -> x1, Pallas kernels: none -> 50.5 us  [shards(): pl.pallas_call(functools.partial(kernel, dims), out_shape=(jax.ShapeDtype...]
    psum x1 -> x0, waiting for transfers between devices: 24.9 us -> none  [shards(): grad_full = lax.psum(grad_flat.astype(jnp.bfloat16), 'sub')]
    reduce_scatter x3 -> x0, waiting for transfers between devices: 22.5 us -> none  [the longest x1 12.5 us: shards(): lax.psum_scatter(grad_b.astype(jnp.bfloat16), 'head', scatter_dimension=0...]
    ppermute x5 -> x0, starting transfers between devices: 16.9 us -> none  [passed_along(): return lax.ppermute(x, axis, pairs)]
    convert_element_type x7 -> x0, local copies, waits for them, and re-layouts: 13.8 us -> none  [the longest x1 4 us: shards(): jnp.dot(inputs, w_in, preferred_element_type=jnp.float32)]
    reshape x3 -> x0, local copies, waits for them, and re-layouts: 5.51 us -> none  [the longest x2 4.53 us: shards(): arrived = arrived_flat.reshape(head_group, state_part, head_width)]
    ppermute x5 -> x0, waiting for transfers between devices: 5.24 us -> none  [passed_along(): return lax.ppermute(x, axis, pairs)]
  transfers between devices with their start and end apart: 9 -> 0, of which waited for: 5 -> 0; matrix products, arithmetic and copies ran while one was open for 40% -> 0% of each run, Pallas kernels for 0% -> 0%
where the time goes in v1:
time: 60.4 us; the launch traced here: 59.3 us
  Pallas kernels  50.5 us (84%)
  local copies, waits for them, and re-layouts  8.15 us (13%)
  between operations  0.64 us (1%)
    pallas_call x1, Pallas kernels, shards(): pl.pallas_call(functools.partial(kernel, dims), out_shape=(jax.ShapeDtype...  50.5 us
    unnamed x3, local copies, waits for them, and re-layouts  5.06 us
    pallas_call x2, local copies, waits for them, and re-layouts, shards(): pl.pallas_call(functools.partial(kernel, dims), out_shape=(jax.ShapeDtype...  3.08 us

profile of v1, /device:TPU:0, one launch (start us, length us, event | category | flops | bytes accessed | tf_op | source)
XLA Modules:
  0.0 59.3 jit_solution(5686543586267058546)
XLA Ops:
  0.6 1.6 %copy.10.b_ref = bf16[512,64]{1,0:T(8,128)(2,1)} copy(bf16[512,64]{0,1:T(8,128)(2,1)} %param.9) | data formatting | bytes 131072 | tf_op args[2]
  2.2 1.6 %copy.11.c_ref = bf16[512,64]{1,0:T(8,128)(2,1)} copy(bf16[512,64]{0,1:T(8,128)(2,1)} %param.10) | data formatting | bytes 131072 | tf_op args[3]
  3.8 50.5 %shard_map.94 = (bf16[512,512]{1,0:T(8,128)(2,1)}, bf16[256,64]{1,0:T(8,128)(2,1)}, bf16[256,64]{1,0:T(8,128)(2,1)}) custom-call(bf16[512,2048]{1,0:T(8,128)(2,1)} %x_hbm.1, bf16[2048,2048]{1,0:T(8,128)(2,1)} %w_hbm.1, bf16[512,2048]{1,0:T(8,128)(2,1)} %g_hbm.1, bf16[512,64]{1,0:T(8,128)(2,1)} %copy.10.b_ref, bf16[512,64]{1,0:T(8,128)(2,1)} %copy.11.c_ref, ...), custom_call_target="tpu_custom_call" | custom-call | tf_op jit(solution)/shard_map/pallas_call | solution.py:402
  54.4 1.5 %copy.12 = bf16[256,64]{0,1:T(8,128)(2,1)} copy(bf16[256,64]{1,0:T(8,128)(2,1)} %get-tuple-element.4) | data formatting | bytes 65536 | tf_op jit(solution)/shard_map/pallas_call | solution.py:402
  55.9 1.5 %copy.13 = bf16[256,64]{0,1:T(8,128)(2,1)} copy(bf16[256,64]{1,0:T(8,128)(2,1)} %get-tuple-element.5) | data formatting | bytes 65536 | tf_op jit(solution)/shard_map/pallas_call | solution.py:402
  57.4 1.9 %copy.15 = bf16[512,512]{1,0:T(8,128)(2,1)} copy(bf16[512,512]{1,0:T(8,128)(2,1)} %get-tuple-element.9) | data formatting | bytes 1048576

commit v2 on v1

--- a/solution.py
+++ b/solution.py
@@ -36,7 +36,7 @@
     half, quarter = T // 2, T // 4
     hpc = CHUNK // HD
     nchunk = HP // CHUNK
-    n_half = b_ref.shape[1]
+    n_half = b_ref.shape[0]
     N = n_half * NS
     tok_own = T // NH
     blk = T // RB
@@ -103,6 +103,10 @@
     rest = dec_t - d1.astype(F32)
     d2 = rest.astype(BF16)
     d3 = (rest - d2.astype(F32)).astype(BF16)
+    def halves(v):
+        hi = v.astype(BF16)
+        return jnp.concatenate([hi.astype(F32), v - hi.astype(F32)], axis=1).astype(BF16)
+
     cum_t = mm(tri, d1) + (mm(tri, d2) + mm(tri, d3))
     cum_r = jnp.transpose(jnp.concatenate([cum_t, jnp.zeros((T, 128 - H), F32)], axis=1))
     for c in range(nchunk):
@@ -111,20 +115,20 @@
         cumc_v[c] = cum_t[:, c * hpc:(c + 1) * hpc]
     tot = cum_t[T - 1:T]
     grow = jnp.exp(cum_t)
-    coef_v[0] = jnp.exp(jnp.minimum(tot - cum_t, 0.0))
+    coef_v[0] = halves(jnp.exp(jnp.minimum(tot - cum_t, 0.0)))
     for l in range(LV):
-        coef_v[1 + l] = turned[:, (l + 2) * H:(l + 3) * H] * grow
+        coef_v[1 + l] = halves(turned[:, (l + 2) * H:(l + 3) * H] * grow)
     ref_a = cum_t[half - 1:half]
-    coef_v[1 + LV] = jnp.concatenate([
+    coef_v[1 + LV] = halves(jnp.concatenate([
         jnp.exp(jnp.minimum(ref_a - cum_t[:half], 0.0)),
-        lam_t[half:] * jnp.exp(jnp.minimum(cum_t[half:] - ref_a, 0.0))], axis=0)
+        lam_t[half:] * jnp.exp(jnp.minimum(cum_t[half:] - ref_a, 0.0))], axis=0))
     pieces = []
     for base in (0, half):
         mid = base + quarter
         ref_b = cum_t[mid - 1:mid]
         pieces.append(jnp.exp(jnp.minimum(ref_b - cum_t[base:mid], 0.0)))
         pieces.append(lam_t[mid:mid + quarter] * jnp.exp(jnp.minimum(cum_t[mid:mid + quarter] - ref_b, 0.0)))
-    coef_v[2 + LV] = jnp.concatenate(pieces, axis=0)
+    coef_v[2 + LV] = halves(jnp.concatenate(pieces, axis=0))
 
     def selector(c, dtype):
         h_i = lax.broadcasted_iota(jnp.int32, (H, CHUNK), 0)
@@ -132,10 +136,9 @@
         return jnp.where(h_i == c * hpc + lax.div(l_i, HD), 1.0, 0.0).astype(dtype)
 
     def spread(v, c):
-        sel = selector(c, BF16)
-        hi = v.astype(BF16)
-        lo = (v - hi.astype(F32)).astype(BF16)
-        return mm(hi, sel) + mm(lo, sel)
+        h_i = lax.rem(lax.broadcasted_iota(jnp.int32, (2 * H, CHUNK), 0), H)
+        l_i = lax.broadcasted_iota(jnp.int32, (2 * H, CHUNK), 1)
+        return mm(v, jnp.where(h_i == c * hpc + lax.div(l_i, HD), 1.0, 0.0).astype(BF16))
 
     tot8 = jnp.broadcast_to(tot, (8, H))
     t1 = tot8.astype(BF16)
@@ -177,12 +180,12 @@
 
     for cp in bc_copies:
         cp.wait_recv()
-    b_v[:, :n_half] = b_ref[...]
-    b_v[:, n_half:] = b_oth[...]
-    c_v[:, :n_half] = c_ref[...]
-    c_v[:, n_half:] = c_oth[...]
-    bt_v[...] = jnp.transpose(b_v[...].astype(F32)).astype(BF16)
-    ct_v[...] = jnp.transpose(c_v[...].astype(F32)).astype(BF16)
+    bt_v[:n_half] = b_ref[...]
+    bt_v[n_half:] = b_oth[...]
+    ct_v[:n_half] = c_ref[...]
+    ct_v[n_half:] = c_oth[...]
+    b_v[...] = jnp.transpose(bt_v[...].astype(F32)).astype(BF16)
+    c_v[...] = jnp.transpose(ct_v[...].astype(F32)).astype(BF16)
     loads[0].wait()
 
     def level_grads(l):
@@ -265,25 +268,28 @@
     q_r = lax.broadcasted_iota(jnp.int32, (quarter, quarter), 0)
     q_c = lax.broadcasted_iota(jnp.int32, (quarter, quarter), 1)
 
+    m_c = lax.div(lax.broadcasted_iota(jnp.int32, (quarter, CHUNK), 1), HD)
+    masks = [jnp.where(m_c == j, 1.0, 0.0).astype(BF16) for j in range(hpc)]
+
     @pl.loop(0, nchunk)
     def _(c):
         keep = q_c >= q_r
         for i in range(4):
             sl = slice(i * quarter, (i + 1) * quarter)
             p_b, g_b = p_v[sl, cols(c)], g_v[sl, cols(c)]
+            dots = mm_nt(jnp.concatenate([p_b * m for m in masks], axis=0), g_b)
             zsum = z_v[sl, sl]
-            locals_x = []
+            weights = []
             for j in range(hpc):
-                lanes = slice(j * HD, (j + 1) * HD)
                 row = cumr_v[c, j:j + 1, sl]
                 lam = lam_v[c, j:j + 1, sl]
                 col = cumc_v[c, sl, j:j + 1]
-                dec = jnp.where(keep, jnp.exp(jnp.minimum(row - col, 0.0)) * lam, 0.0)
-                zsum = zsum + dec * mm_nt(p_b[:, lanes], g_b[:, lanes])
-                lwt = (dec * sc_v[sl, sl]).astype(BF16)
-                locals_x.append(mm(lwt, g_b[:, lanes]))
+                dec = jnp.where(keep, jnp.exp(row - col) * lam, 0.0)
+                zsum = zsum + dec * dots[j * quarter:(j + 1) * quarter]
+                weights.append((dec * sc_v[sl, sl]).astype(BF16))
             z_v[sl, sl] = zsum
-            gxl_v[sl, cols(c)] += jnp.concatenate(locals_x, axis=1)
+            gxl_v[sl, cols(c)] += mm(jnp.concatenate(weights, axis=1),
+                                     jnp.concatenate([g_b * m for m in masks], axis=0))
 
     bwd[0][1]()
     if LV > 1:
@@ -341,9 +347,7 @@
                             gbc_sem, n, {"head": k, "sub": lax.rem(sub + ds, NS)})
                 cp.start()
                 gbc_copies.append(cp)
-    for r in range(RB):
-        rs = slice(r * blk, (r + 1) * blk)
-        own_v[rs] = mm_nt(gx_v[0, rs], wb_v[head, :, :HP]) + mm_nt(gx_v[1, rs], wb_v[head, :, HP:])
+    own_v[...] = mm_nt(gx_v[0], wb_v[head, :, :HP]) + mm_nt(gx_v[1], wb_v[head, :, HP:])
     own_tok = pl.ds(pl.multiple_of(head * tok_own, 16), tok_own)
     gb = gbc_s[0, 0, own_tok].astype(F32)
     gc = gbc_s[0, 1, own_tok].astype(F32)
@@ -351,8 +355,9 @@
         cp.wait_recv()
         gb = gb + gbc_r[n, 0].astype(F32)
         gc = gc + gbc_r[n, 1].astype(F32)
-    gb_ref[...] = gb.astype(BF16)
-    gc_ref[...] = gc.astype(BF16)
+    both = jnp.transpose(jnp.concatenate([gb, gc], axis=1))
+    gb_ref[...] = both[:n_half].astype(BF16)
+    gc_ref[...] = both[n_half:].astype(BF16)
     for r in range(RB):
         rs = slice(r * blk, (r + 1) * blk)
         acc = own_v[rs]
@@ -378,15 +383,15 @@
     nh = b_in.shape[1]
     N = nh * NS
     OC = D // NH // NS
-    RB = 4
+    RB = 2
     nchunk = HP // CHUNK
     tok_own = T // NH
     dims = (T, H, HP, HD, NS, NH, NCTX, LV, OC, RB)
     V = pltpu.VMEM
     scratch = [
         V((T, D), BF16), V((D, HP), BF16), V((NH, OC, inner), BF16), V((T, HP), BF16),
-        V((T, nh), BF16), V((T, nh), BF16), V((T, N), BF16), V((T, N), BF16), V((N, T), BF16), V((N, T), BF16),
-        V((LV + 3, T, H), F32), V((nchunk, T, CHUNK // HD), F32), V((nchunk, 8, T), F32), V((nchunk, 8, T), F32),
+        V((nh, T), BF16), V((nh, T), BF16), V((T, N), BF16), V((T, N), BF16), V((N, T), BF16), V((N, T), BF16),
+        V((LV + 3, T, 2 * H), BF16), V((nchunk, T, CHUNK // HD), F32), V((nchunk, 8, T), F32), V((nchunk, 8, T), F32),
         V((LV, 8, HP), F32), V((LV, 8, HP), F32), V((LV, 8, HP), F32),
         V((LV, T, HP), BF16), V((T, HP), BF16), V((T, HP), BF16), V((LV, N, HP), F32), V((N, HP), F32),
         V((LV, N, HP), BF16), V((LV, N, HP), BF16), V((LV, N, HP), BF16), V((LV, N, HP), BF16), V((N, HP), F32),
@@ -399,16 +404,17 @@
                 S((2, (NH - 1) * RB)), S((2, NH * NS - 1))]
     vm = pl.BlockSpec(memory_space=pltpu.VMEM)
     hb = pl.BlockSpec(memory_space=pl.ANY)
-    return pl.pallas_call(
+    grad_inputs, grad_b, grad_c = pl.pallas_call(
         functools.partial(kernel, dims),
-        out_shape=(jax.ShapeDtypeStruct((T, OC), BF16), jax.ShapeDtypeStruct((tok_own, nh), BF16),
-                   jax.ShapeDtypeStruct((tok_own, nh), BF16)),
+        out_shape=(jax.ShapeDtypeStruct((T, OC), BF16), jax.ShapeDtypeStruct((nh, tok_own), BF16),
+                   jax.ShapeDtypeStruct((nh, tok_own), BF16)),
         in_specs=[hb, hb, hb, vm, vm, vm, vm],
         out_specs=(vm, vm, vm),
         scratch_shapes=scratch,
         compiler_params=pltpu.CompilerParams(
             collective_id=0, has_side_effects=True, vmem_limit_bytes=56 * 2 ** 20),
-    )(inputs, w_in, out_grad, b_in, c_in, log_decay, level_weight)
+    )(inputs, w_in, out_grad, b_in.T, c_in.T, log_decay, level_weight)
+    return grad_inputs, grad_b.T, grad_c.T
 
 
 def solution(mesh):

time: 60.4 us -> 58.9 us (0.975)
  the two profiles are of different devices: /device:TPU:0 before, /device:TPU:8 now
where the time goes in v2:
time: 58.9 us; the launch traced here: 58.6 us
  Pallas kernels  53.3 us (90%)
  local copies, waits for them, and re-layouts  4.62 us (8%)
  between operations  0.64 us (1%)
    pallas_call x1, Pallas kernels, shards(): pl.pallas_call(functools.partial(kernel, dims), out_shape=(jax.ShapeDtype...  53.3 us
    unnamed x3, local copies, waits for them, and re-layouts  4.62 us

profile of v2, /device:TPU:8, one launch (start us, length us, event | category | flops | bytes accessed | tf_op | source)
XLA Modules:
  0.0 58.6 jit_solution(6497929306805062708)
XLA Ops:
  0.6 53.3 %shard_map.94 = (bf16[512,512]{1,0:T(8,128)(2,1)}, bf16[64,256]{1,0:T(8,128)(2,1)}, bf16[64,256]{1,0:T(8,128)(2,1)}) custom-call(bf16[512,2048]{1,0:T(8,128)(2,1)} %x_hbm.1, bf16[2048,2048]{1,0:T(8,128)(2,1)} %w_hbm.1, bf16[512,2048]{1,0:T(8,128)(2,1)} %g_hbm.1, bf16[64,512]{1,0:T(8,128)(2,1)} %bitcast.4, bf16[64,512]{1,0:T(8,128)(2,1)} %bitcast.5, ...), custom_call_target="tpu_custom_call" | custom-call | tf_op jit(solution)/shard_map/pallas_call | solution.py:407
  54.0 1.9 %copy.13 = bf16[512,512]{1,0:T(8,128)(2,1)} copy(bf16[512,512]{1,0:T(8,128)(2,1)} %get-tuple-element.12) | data formatting | bytes 1048576
  55.8 1.4 %copy.14 = bf16[256,64]{0,1:T(8,128)(2,1)} copy(bf16[256,64]{0,1:T(8,128)(2,1)} %bitcast.7) | data formatting | bytes 65536
  57.2 1.4 %copy.15 = bf16[256,64]{0,1:T(8,128)(2,1)} copy(bf16[256,64]{0,1:T(8,128)(2,1)} %bitcast.6) | data formatting | bytes 65536

commit v3 on v2

--- a/solution.py
+++ b/solution.py
@@ -205,6 +205,9 @@
     ret_s[LV - 1] = (a_v[LV - 1] * jnp.exp(gap[LV - 1, 0:1])).astype(BF16)
     bwd[LV - 1][0]()
 
+    for l in range(LV - 1):
+        level_grads(l)
+
     loads[1].wait()
     loads[2].wait()
 
@@ -219,8 +222,6 @@
         win_s[0, :, cols(c)] = e.astype(BF16)
 
     fwd[0][0]()
-    for l in range(LV - 1):
-        level_grads(l)
 
     sc_v[...] = mm_nt(b_v[...], c_v[...])
     scb_v[...] = sc_v[...].astype(BF16)
@@ -244,14 +245,7 @@
         gxl_v[half:half + quarter, cols(c)] = near_b
         gxl_v[quarter * 3:, cols(c)] = jnp.zeros((quarter, CHUNK), F32)
 
-    state = [None]
-
-    def ladder(l):
-        fwd[l][1]()
-        keep = e_v[...] if l == 0 else e_v[...]
-        e_v[...] = keep + jnp.exp(wlog[l, 0:1]) * arr_v[l].astype(F32)
-        win_s[l + 1] = e_v[...].astype(BF16)
-        fwd[l + 1][0]()
+    for l in range(LV - 1):
         k = LV - 1 - l
         bwd[k][1]()
         if l == 0:
@@ -261,9 +255,10 @@
         ret_s[k - 1] = (a_v[k - 1] * jnp.exp(gap[k - 1, 0:1])
                         + jnp.exp(wlog[k - 1, 0:1]) * sg_v[...]).astype(BF16)
         bwd[k - 1][0]()
-
-    for l in range(LV - 1):
-        ladder(l)
+        fwd[l][1]()
+        e_v[...] += jnp.exp(wlog[l, 0:1]) * arr_v[l].astype(F32)
+        win_s[l + 1] = e_v[...].astype(BF16)
+        fwd[l + 1][0]()
 
     q_r = lax.broadcasted_iota(jnp.int32, (quarter, quarter), 0)
     q_c = lax.broadcasted_iota(jnp.int32, (quarter, quarter), 1)
@@ -271,25 +266,29 @@
     m_c = lax.div(lax.broadcasted_iota(jnp.int32, (quarter, CHUNK), 1), HD)
     masks = [jnp.where(m_c == j, 1.0, 0.0).astype(BF16) for j in range(hpc)]
 
-    @pl.loop(0, nchunk)
-    def _(c):
-        keep = q_c >= q_r
-        for i in range(4):
-            sl = slice(i * quarter, (i + 1) * quarter)
-            p_b, g_b = p_v[sl, cols(c)], g_v[sl, cols(c)]
-            dots = mm_nt(jnp.concatenate([p_b * m for m in masks], axis=0), g_b)
-            zsum = z_v[sl, sl]
-            weights = []
-            for j in range(hpc):
-                row = cumr_v[c, j:j + 1, sl]
-                lam = lam_v[c, j:j + 1, sl]
-                col = cumc_v[c, sl, j:j + 1]
-                dec = jnp.where(keep, jnp.exp(row - col) * lam, 0.0)
-                zsum = zsum + dec * dots[j * quarter:(j + 1) * quarter]
-                weights.append((dec * sc_v[sl, sl]).astype(BF16))
-            z_v[sl, sl] = zsum
-            gxl_v[sl, cols(c)] += mm(jnp.concatenate(weights, axis=1),
-                                     jnp.concatenate([g_b * m for m in masks], axis=0))
+    keep = q_c >= q_r
+
+    def diagonal(blocks):
+        @pl.loop(0, nchunk)
+        def _(c):
+            for i in blocks:
+                sl = slice(i * quarter, (i + 1) * quarter)
+                p_b, g_b = p_v[sl, cols(c)], g_v[sl, cols(c)]
+                dots = mm_nt(jnp.concatenate([p_b * m for m in masks], axis=0), g_b)
+                zsum = z_v[sl, sl]
+                weights = []
+                for j in range(hpc):
+                    row = cumr_v[c, j:j + 1, sl]
+                    lam = lam_v[c, j:j + 1, sl]
+                    col = cumc_v[c, sl, j:j + 1]
+                    dec = jnp.where(keep, jnp.exp(row - col) * lam, 0.0)
+                    zsum = zsum + dec * dots[j * quarter:(j + 1) * quarter]
+                    weights.append((dec * sc_v[sl, sl]).astype(BF16))
+                z_v[sl, sl] = zsum
+                gxl_v[sl, cols(c)] += mm(jnp.concatenate(weights, axis=1),
+                                         jnp.concatenate([g_b * m for m in masks], axis=0))
+
+    diagonal((0, 1))
 
     bwd[0][1]()
     if LV > 1:
@@ -298,8 +297,9 @@
         sg_v[...] = came_v[0].astype(F32)
     sgb = sg_v[...].astype(BF16)
     came_v[0] = sgb
-    gx_copies = []
-    for r in range(RB):
+    gx_copies, part_copies = [], []
+
+    def send_rows(r):
         rs = slice(r * blk, (r + 1) * blk)
 
         @pl.loop(0, nchunk)
@@ -312,15 +312,11 @@
         cp.start()
         gx_copies.append(cp)
 
-    for k in range(NH):
-        loads[3 + k].wait()
-    part_copies = []
-    for r in range(RB):
+    def send_parts(r):
         rs = slice(r * blk, (r + 1) * blk)
         gx_copies[r].wait_recv()
         for d in range(1, NH):
             k = lax.rem(head + d, NH)
-
             part = mm_nt(gx_v[0, rs], wb_v[k, :, :HP]) + mm_nt(gx_v[1, rs], wb_v[k, :, HP:])
             part_s[d - 1, rs] = part.astype(BF16)
             cp = remote(part_s.at[d - 1, pl.ds(r * blk, blk)], part_r.at[d - 1, pl.ds(r * blk, blk)],
@@ -328,9 +324,17 @@
             cp.start()
             part_copies.append(cp)
 
-    fwd[LV - 1][1]()
+    send_rows(0)
+    diagonal((2, 3))
+    for k in range(NH):
+        loads[3 + k].wait()
+    send_parts(0)
+    send_rows(1)
     gb_all = mm(z_v[...].astype(BF16), c_v[...]) + mm_nt(pe_v[...], came_v[0])
     gc_all = mm(jnp.transpose(z_v[...]).astype(BF16), b_v[...])
+    send_parts(1)
+
+    fwd[LV - 1][1]()
     for l in range(LV):
         gc_all = gc_all + mm_nt(gl_v[l], (arr_v[l].astype(F32) * jnp.exp(gap[l, 0:1])).astype(BF16))
     gbc_copies = []
@@ -370,6 +374,11 @@
         cp.wait_send()
     for mv in log_moves + fwd + bwd:
         mv[2]()
+
+
+def hand_out(*refs):
+    for src, dst in zip(refs[:3], refs[3:]):
+        dst[...] = src[...]
 
 
 def shards(inputs, w_in, b_in, c_in, log_decay, level_weight, out_grad):
@@ -414,6 +423,10 @@
         compiler_params=pltpu.CompilerParams(
             collective_id=0, has_side_effects=True, vmem_limit_bytes=56 * 2 ** 20),
     )(inputs, w_in, out_grad, b_in.T, c_in.T, log_decay, level_weight)
+    outs = (grad_inputs, grad_b, grad_c)
+    grad_inputs, grad_b, grad_c = pl.pallas_call(
+        hand_out, out_shape=tuple(jax.ShapeDtypeStruct(o.shape, o.dtype) for o in outs),
+        in_specs=[vm] * 3, out_specs=(vm,) * 3)(*outs)
     return grad_inputs, grad_b.T, grad_c.T
 
 

time: 58.9 us -> 54.4 us (0.924)
  the two profiles are of different devices: /device:TPU:8 before, /device:TPU:0 now
where the time goes in v3:
time: 54.4 us; the launch traced here: 54.2 us
  Pallas kernels  53.6 us (99%)
  between operations  0.64 us (1%)
    pallas_call x1, Pallas kernels, shards(): pl.pallas_call(functools.partial(kernel, dims), out_shape=(jax.ShapeDtype...  51.7 us
    pallas_call x1, Pallas kernels, shards(): pl.pallas_call(hand_out, out_shape=tuple((jax.ShapeDtypeStruct(o.shape, o...  1.9 us

profile of v3, /device:TPU:0, one launch (start us, length us, event | category | flops | bytes accessed | tf_op | source)
XLA Modules:
  0.0 54.2 jit_solution(9444081082574430441)
XLA Ops:
  0.6 51.7 %shard_map.94 = (bf16[512,512]{1,0:T(8,128)(2,1)}, bf16[64,256]{1,0:T(8,128)(2,1)}, bf16[64,256]{1,0:T(8,128)(2,1)}) custom-call(bf16[512,2048]{1,0:T(8,128)(2,1)} %x_hbm.1, bf16[2048,2048]{1,0:T(8,128)(2,1)} %w_hbm.1, bf16[512,2048]{1,0:T(8,128)(2,1)} %g_hbm.1, bf16[64,512]{1,0:T(8,128)(2,1)} %bitcast.4, bf16[64,512]{1,0:T(8,128)(2,1)} %bitcast.5, ...), custom_call_target="tpu_custom_call" | custom-call | tf_op jit(solution)/shard_map/pallas_call | solution.py:416
  52.3 1.9 %shard_map.95 = (bf16[512,512]{1,0:T(8,128)(2,1)}, bf16[64,256]{1,0:T(8,128)(2,1)}, bf16[64,256]{1,0:T(8,128)(2,1)}) custom-call(bf16[512,512]{1,0:T(8,128)(2,1)} %get-tuple-element.9.refs_0_, bf16[64,256]{1,0:T(8,128)(2,1)} %get-tuple-element.10.refs_1_, bf16[64,256]{1,0:T(8,128)(2,1)} %get-tuple-element.11.refs_2_), custom_call_target="tpu_custom_call" | custom-call | tf_op jit(solution)/shard_map/pallas_call | solution.py:427

commit v4 on v3

--- a/solution.py
+++ b/solution.py
@@ -56,7 +56,7 @@
     for k in range(NH):
         loads.append(pltpu.make_async_copy(
             w_hbm.at[pl.ds(pl.multiple_of((k * NS + sub) * OC, 128), OC), :], wb_v.at[k], ld_sem.at[3 + k]))
-    for ld in loads:
+    for ld in loads[:3]:
         ld.start()
 
     barrier = pltpu.get_barrier_semaphore()
@@ -210,6 +210,8 @@
 
     loads[1].wait()
     loads[2].wait()
+    for ld in loads[3:]:
+        ld.start()
 
     @pl.loop(0, nchunk)
     def _(c):
@@ -244,21 +246,6 @@
         gxl_v[:quarter, cols(c)] += near_a
         gxl_v[half:half + quarter, cols(c)] = near_b
         gxl_v[quarter * 3:, cols(c)] = jnp.zeros((quarter, CHUNK), F32)
-
-    for l in range(LV - 1):
-        k = LV - 1 - l
-        bwd[k][1]()
-        if l == 0:
-            sg_v[...] = came_v[k].astype(F32)
-        else:
-            sg_v[...] += came_v[k].astype(F32)
-        ret_s[k - 1] = (a_v[k - 1] * jnp.exp(gap[k - 1, 0:1])
-                        + jnp.exp(wlog[k - 1, 0:1]) * sg_v[...]).astype(BF16)
-        bwd[k - 1][0]()
-        fwd[l][1]()
-        e_v[...] += jnp.exp(wlog[l, 0:1]) * arr_v[l].astype(F32)
-        win_s[l + 1] = e_v[...].astype(BF16)
-        fwd[l + 1][0]()
 
     q_r = lax.broadcasted_iota(jnp.int32, (quarter, quarter), 0)
     q_c = lax.broadcasted_iota(jnp.int32, (quarter, quarter), 1)
@@ -288,7 +275,24 @@
                 gxl_v[sl, cols(c)] += mm(jnp.concatenate(weights, axis=1),
                                          jnp.concatenate([g_b * m for m in masks], axis=0))
 
-    diagonal((0, 1))
+    for l in range(LV - 1):
+        k = LV - 1 - l
+        bwd[k][1]()
+        if l == 0:
+            sg_v[...] = came_v[k].astype(F32)
+        else:
+            sg_v[...] += came_v[k].astype(F32)
+        ret_s[k - 1] = (a_v[k - 1] * jnp.exp(gap[k - 1, 0:1])
+                        + jnp.exp(wlog[k - 1, 0:1]) * sg_v[...]).astype(BF16)
+        bwd[k - 1][0]()
+        if l == 0:
+            diagonal((0, 1))
+        fwd[l][1]()
+        e_v[...] += jnp.exp(wlog[l, 0:1]) * arr_v[l].astype(F32)
+        win_s[l + 1] = e_v[...].astype(BF16)
+        fwd[l + 1][0]()
+    if LV == 1:
+        diagonal((0, 1))
 
     bwd[0][1]()
     if LV > 1:

time: 54.4 us -> 54.4 us (level)
  no operation moved by 1% of the time
where the time goes in v4:
time: 54.4 us; the launch traced here: 54.2 us
  Pallas kernels  53.6 us (99%)
  between operations  0.64 us (1%)
    pallas_call x1, Pallas kernels, shards(): pl.pallas_call(functools.partial(kernel, dims), out_shape=(jax.ShapeDtype...  51.7 us
    pallas_call x1, Pallas kernels, shards(): pl.pallas_call(hand_out, out_shape=tuple((jax.ShapeDtypeStruct(o.shape, o...  1.9 us

profile of v4, /device:TPU:0, one launch (start us, length us, event | category | flops | bytes accessed | tf_op | source)
XLA Modules:
  0.0 54.2 jit_solution(10902614623466361876)
XLA Ops:
  0.6 51.7 %shard_map.94 = (bf16[512,512]{1,0:T(8,128)(2,1)}, bf16[64,256]{1,0:T(8,128)(2,1)}, bf16[64,256]{1,0:T(8,128)(2,1)}) custom-call(bf16[512,2048]{1,0:T(8,128)(2,1)} %x_hbm.1, bf16[2048,2048]{1,0:T(8,128)(2,1)} %w_hbm.1, bf16[512,2048]{1,0:T(8,128)(2,1)} %g_hbm.1, bf16[64,512]{1,0:T(8,128)(2,1)} %bitcast.4, bf16[64,512]{1,0:T(8,128)(2,1)} %bitcast.5, ...), custom_call_target="tpu_custom_call" | custom-call | tf_op jit(solution)/shard_map/pallas_call | solution.py:420
  52.3 1.9 %shard_map.95 = (bf16[512,512]{1,0:T(8,128)(2,1)}, bf16[64,256]{1,0:T(8,128)(2,1)}, bf16[64,256]{1,0:T(8,128)(2,1)}) custom-call(bf16[512,512]{1,0:T(8,128)(2,1)} %get-tuple-element.9.refs_0_, bf16[64,256]{1,0:T(8,128)(2,1)} %get-tuple-element.10.refs_1_, bf16[64,256]{1,0:T(8,128)(2,1)} %get-tuple-element.11.refs_2_), custom_call_target="tpu_custom_call" | custom-call | tf_op jit(solution)/shard_map/pallas_call | solution.py:431

commit v5 on v4

--- a/solution.py
+++ b/solution.py
@@ -329,14 +329,18 @@
             part_copies.append(cp)
 
     send_rows(0)
+    send_rows(1)
     diagonal((2, 3))
     for k in range(NH):
         loads[3 + k].wait()
     send_parts(0)
-    send_rows(1)
+    send_parts(1)
+    send_rows(2)
+    send_rows(3)
     gb_all = mm(z_v[...].astype(BF16), c_v[...]) + mm_nt(pe_v[...], came_v[0])
     gc_all = mm(jnp.transpose(z_v[...]).astype(BF16), b_v[...])
-    send_parts(1)
+    send_parts(2)
+    send_parts(3)
 
     fwd[LV - 1][1]()
     for l in range(LV):
@@ -396,7 +400,7 @@
     nh = b_in.shape[1]
     N = nh * NS
     OC = D // NH // NS
-    RB = 2
+    RB = 4
     nchunk = HP // CHUNK
     tok_own = T // NH
     dims = (T, H, HP, HD, NS, NH, NCTX, LV, OC, RB)

time: 54.4 us -> 54.9 us (level)
    pallas_call x1, Pallas kernels: 51.7 us -> 52.2 us  [shards(): pl.pallas_call(functools.partial(kernel, dims), out_shape=(jax.ShapeDtype...]
where the time goes in v5:
time: 54.9 us; the launch traced here: 54.7 us
  Pallas kernels  54.1 us (99%)
  between operations  0.64 us (1%)
    pallas_call x1, Pallas kernels, shards(): pl.pallas_call(functools.partial(kernel, dims), out_shape=(jax.ShapeDtype...  52.2 us
    pallas_call x1, Pallas kernels, shards(): pl.pallas_call(hand_out, out_shape=tuple((jax.ShapeDtypeStruct(o.shape, o...  1.9 us

profile of v5, /device:TPU:0, one launch (start us, length us, event | category | flops | bytes accessed | tf_op | source)
XLA Modules:
  0.0 54.7 jit_solution(3222202681585302769)
XLA Ops:
  0.6 52.2 %shard_map.94 = (bf16[512,512]{1,0:T(8,128)(2,1)}, bf16[64,256]{1,0:T(8,128)(2,1)}, bf16[64,256]{1,0:T(8,128)(2,1)}) custom-call(bf16[512,2048]{1,0:T(8,128)(2,1)} %x_hbm.1, bf16[2048,2048]{1,0:T(8,128)(2,1)} %w_hbm.1, bf16[512,2048]{1,0:T(8,128)(2,1)} %g_hbm.1, bf16[64,512]{1,0:T(8,128)(2,1)} %bitcast.4, bf16[64,512]{1,0:T(8,128)(2,1)} %bitcast.5, ...), custom_call_target="tpu_custom_call" | custom-call | tf_op jit(solution)/shard_map/pallas_call | solution.py:424
  52.9 1.9 %shard_map.95 = (bf16[512,512]{1,0:T(8,128)(2,1)}, bf16[64,256]{1,0:T(8,128)(2,1)}, bf16[64,256]{1,0:T(8,128)(2,1)}) custom-call(bf16[512,512]{1,0:T(8,128)(2,1)} %get-tuple-element.9.refs_0_, bf16[64,256]{1,0:T(8,128)(2,1)} %get-tuple-element.10.refs_1_, bf16[64,256]{1,0:T(8,128)(2,1)} %get-tuple-element.11.refs_2_), custom_call_target="tpu_custom_call" | custom-call | tf_op jit(solution)/shard_map/pallas_call | solution.py:435
